TPU v7x, 32 devices: a whole 2x2x4 slice. The times are simulated.
32 devices in a mesh: fsdp: 8 (over y, x, core), tensor: 4 (over z).
Axes of the slice: x: 2, y: 2, z: 4, core: 2. Of those that a mesh axis runs over, the one named last changes fastest.
Arguments:
- hidden_t: bfloat16 [28672, 512], P('fsdp', 'tensor'), may hold values from -6 to 6
- down_weight: bfloat16 [28672, 4096], P('fsdp', 'tensor'), may hold values from -0.03125 to 0.03125
- probe: bfloat16 [28672, 4096], P('fsdp', 'tensor'), may hold values from -5 to 5
- grad_moment: bfloat16 [28672, 4096], P('fsdp', 'tensor'), may hold values from -0.0059814453 to 0.0059814453
- curv_moment: bfloat16 [28672, 4096], P('fsdp', 'tensor'), may hold values from 0.0099487305 to 0.099609375
- target: bfloat16 [512, 4096], P('fsdp', 'tensor'), may hold values from -6 to 6
Outputs:
- new_grad_moment: bfloat16 [28672, 4096], P('fsdp', 'tensor')
- new_curv_moment: bfloat16 [28672, 4096], P('fsdp', 'tensor')
- update: bfloat16 [28672, 4096], P('fsdp', 'tensor')
All inputs are finite; a program needn't handle non-finite values.
Results may differ from a plain program's by a relative error of at most 0.0056.
Values may be sent and summed in bfloat16 or wider, within the bound.
A program may use at most 192 MiB of HBM per device.

v0:
```python
import jax
import jax.numpy as jnp
from jax import lax
from jax.sharding import PartitionSpec as P

BETA_ONE = 0.965
BETA_TWO = 0.99
RHO_SCALE = 0.02
EPS_FLOOR = 0.0005


def cotangents(summed, target_rows, col_width, token_count):
    adjoint = ((summed[:, :col_width] - target_rows.astype(jnp.float32)) / token_count).astype(
        jnp.bfloat16
    )
    tangent_adjoint = (summed[:, col_width:] / token_count).astype(jnp.bfloat16)
    return jnp.concatenate([adjoint, tangent_adjoint], axis=1)


def shards(hidden_t, down_weight, probe, grad_moment, curv_moment, target):
    gathered = lax.all_gather(hidden_t, "tensor", axis=1, tiled=True)
    col_width = down_weight.shape[1]
    token_count = gathered.shape[1]
    paired = jnp.concatenate([down_weight, probe], axis=1)
    partial_out = lax.dot_general(
        gathered, paired, (((0,), (0,)), ((), ())), preferred_element_type=jnp.float32
    )
    totals = lax.psum(partial_out, "fsdp")
    target_all = lax.all_gather(target, "fsdp", axis=0, tiled=True)
    stacked = cotangents(totals, target_all, col_width, token_count)
    products = jnp.dot(gathered, stacked, preferred_element_type=jnp.float32)
    gradient = products[:, :col_width]
    hess_probe = products[:, col_width:]
    estimate = probe.astype(jnp.float32) * hess_probe
    moment_next = BETA_ONE * grad_moment.astype(jnp.float32) + (1.0 - BETA_ONE) * gradient
    curv_next = BETA_TWO * curv_moment.astype(jnp.float32) + (1.0 - BETA_TWO) * estimate
    raw_ratio = moment_next / jnp.maximum(RHO_SCALE * curv_next, EPS_FLOOR)
    update = jnp.clip(raw_ratio, -1.0, 1.0)
    return (
        moment_next.astype(jnp.bfloat16),
        curv_next.astype(jnp.bfloat16),
        update.astype(jnp.bfloat16),
    )


def solution(mesh):
    in_specs = (
        P("fsdp", "tensor"),
        P("fsdp", "tensor"),
        P("fsdp", "tensor"),
        P("fsdp", "tensor"),
        P("fsdp", "tensor"),
        P("fsdp", "tensor"),
    )
    out_specs = (P("fsdp", "tensor"), P("fsdp", "tensor"), P("fsdp", "tensor"))
    return jax.shard_map(shards, mesh=mesh, in_specs=in_specs, out_specs=out_specs, check_vma=False)
```

profile of v0, /device:TPU:0, one launch (start us, length us, event | category | flops | bytes accessed | tf_op | source)
XLA Modules:
  0.0 273.3 jit_solution(6230435863053550682)
XLA Ops:
  7.2 0.0 all-gather.3.cloned.1.call-start
  7.2 0.7 all-gather.3.cloned.1.call-update
  7.9 0.0 all-gather.5.cloned.1.call-start
  7.9 0.7 all-gather.5.cloned.1.call-update
  8.6 0.0 all-reduce.2.cloned.1.call-start
  8.7 75.6 %all-gather.3.cloned.1.call-done = bf16[3584,512]{1,0:T(8,128)(2,1)} async-done(((bf16[3584,128]{1,0:T(8,128)(2,1)}), bf16[3584,512]{1,0:T(8,128)(2,1)}) %all-gather.3.cloned.1.call-update) | async-done | bytes 3670032 | tf_op jit(solution)/shard_map/all_gather | solution.py:21
  84.3 16.0 %fusion.8 = f32[512,2048]{0,1:T(8,128)} fusion(bf16[3584,512]{1,0:T(8,128)(2,1)} %all-gather.3.cloned.1.call-done, bf16[3584,1024]{1,0:T(8,128)(2,1)} %param.8, bf16[3584,1024]{1,0:T(8,128)(2,1)} %param.7), kind=kOutput, calls=%fused_computation.12 | convolution fusion | flops 7545552896 | bytes 22544384 | tf_op jit(solution)/shard_map/dot_general | solution.py:25
  100.3 0.0 all-reduce.2.cloned.1.call-update
  100.3 10.2 %copy.19 = bf16[3584,1024]{0,1:T(8,128)(2,1)} copy(bf16[3584,1024]{1,0:T(8,128)(2,1)} %param.8) | data formatting | bytes 14680064 | tf_op args[2]
  110.6 10.2 %copy.16 = bf16[3584,1024]{0,1:T(8,128)(2,1)} copy(bf16[3584,1024]{1,0:T(8,128)(2,1)} %param.9) | data formatting | bytes 14680064 | tf_op args[3]
  120.7 10.0 %copy.18 = bf16[3584,1024]{0,1:T(8,128)(2,1)} copy(bf16[3584,1024]{1,0:T(8,128)(2,1)} %param.10) | data formatting | bytes 14680064 | tf_op args[4]
  130.8 0.0 all-gather.5.cloned.1.call-done
  130.8 1.5 copy.17
  132.3 59.9 %all-reduce.2.cloned.1.call-done = f32[512,2048]{0,1:T(8,128)} async-done(((f32[512,2048]{0,1:T(8,128)}), f32[512,2048]{0,1:T(8,128)}) %all-reduce.2.cloned.1.call-update) | async-done | bytes 4194320 | tf_op jit(solution)/shard_map/psum | solution.py:28
  192.2 0.0 slice-start
  192.2 3.0 %fusion.14 = (bf16[512,1024]{0,1:T(8,128)(2,1)S(1)}, bf16[512,1024]{0,1:T(8,128)(2,1)S(1)}) fusion(f32[512,2048]{0,1:T(8,128)} %all-reduce.2.cloned.1.call-done, bf16[512,1024]{0,1:T(8,128)(2,1)S(1)} %copy.17), kind=kLoop, calls=%fused_computation.18 | loop fusion | flops 3145728 | bytes 7340032 | tf_op jit(solution)/shard_map/convert_element_type | solution.py:13
  195.2 0.0 slice-start.1
  195.3 16.8 %convolution_bitcast_fusion = f32[3584,2048]{0,1:T(8,128)} fusion(bf16[3584,512]{1,0:T(8,128)(2,1)} %all-gather.3.cloned.1.call-done, bf16[512,1024]{0,1:T(8,128)(2,1)S(1)} %get-tuple-element.13, bf16[512,1024]{0,1:T(8,128)(2,1)S(1)} %get-tuple-element.12), kind=kOutput, calls=%fused_computation | convolution fusion | flops 7520387072 | bytes 35127296 | tf_op jit(solution)/shard_map/dot_general | solution.py:31
  212.1 0.0 slice-done
  212.1 0.0 slice-done.1
  212.1 23.6 %clamp_convert_fusion = (bf16[3584,1024]{0,1:T(8,128)(2,1)}, bf16[3584,1024]{0,1:T(8,128)(2,1)}, bf16[3584,1024]{0,1:T(8,128)(2,1)}) fusion(f32[3584,2048]{0,1:T(8,128)} %convolution_bitcast_fusion, bf16[3584,1024]{0,1:T(8,128)(2,1)} %copy.16, bf16[3584,1024]{0,1:T(8,128)(2,1)S(1)} %bitcast.7, bf16[3584,1024]{0,1:T(8,128)(2,1)} %copy.18), kind=kLoop, calls=%fused_computation.10 | loop fusion | flops 62390272 | bytes 73400320 | tf_op jit(solution)/shard_map/convert_element_type | solution.py:42
  235.6 10.4 %copy.20 = bf16[3584,1024]{1,0:T(8,128)(2,1)} copy(bf16[3584,1024]{0,1:T(8,128)(2,1)} %get-tuple-element.11) | data formatting | bytes 14680064
  246.0 10.4 %copy.21 = bf16[3584,1024]{1,0:T(8,128)(2,1)} copy(bf16[3584,1024]{0,1:T(8,128)(2,1)} %get-tuple-element.10) | data formatting | bytes 14680064
  256.4 10.4 %copy.22 = bf16[3584,1024]{1,0:T(8,128)(2,1)} copy(bf16[3584,1024]{0,1:T(8,128)(2,1)} %get-tuple-element.9) | data formatting | bytes 14680064
  (1 shorter events, 0.0 us)
Async XLA Ops:
  7.2 77.1 %all-gather.3.cloned.1.call-start = ((), (), s32[]{:S(2)}) async-start(), calls=%async_computation | async-start | bytes 4587520 | tf_op jit(solution)/shard_map/all_gather | solution.py:21
  7.9 122.9 %all-gather.5.cloned.1.call-start = ((), (), s32[]{:S(2)}) async-start(), calls=%async_computation.2 | async-start | bytes 1179648 | tf_op jit(solution)/shard_map/all_gather | solution.py:29
  8.6 183.6 %all-reduce.2.cloned.1.call-start = ((), (), s32[]{:S(2)}) async-start(), calls=%async_computation.1 | async-start | bytes 8388608 | tf_op jit(solution)/shard_map/psum | solution.py:28
  192.2 19.9 %slice-start = ((s8[7340032]{0:T(1024)(128)(4,1)}), s8[4194304]{0:T(1024)(128)(4,1)S(1)}, s32[]{:S(2)}) async-start(s8[7340032]{0:T(1024)(128)(4,1)} %bitcast.6), calls=%async_computation.3 | async-start | bytes 8388608
  195.2 16.8 %slice-start.1 = ((s8[7340032]{0:T(1024)(128)(4,1)}), s8[3145728]{0:T(1024)(128)(4,1)S(1)}, s32[]{:S(2)}) async-start(s8[7340032]{0:T(1024)(128)(4,1)} %bitcast.6), calls=%async_computation.4 | async-start | bytes 6291456
Sparse Core Ops, SparseCore 0:
  9.6 74.6 all-gather.2
  86.2 21.6 all-gather.4
  111.2 80.9 all-reduce.1
where the time goes:
time: 275 us; the launch traced here: 273 us
  waiting for transfers between devices  137 us (50%)
  local copies, waits for them, and re-layouts  63.2 us (23%)
  matrix products  32.8 us (12%)
  other arithmetic  26.6 us (10%)
  between operations  13.8 us (5%)
    all_gather x1, waiting for transfers between devices, shards(): gathered = lax.all_gather(hidden_t, 'tensor', axis=1, tiled=True)  75.6 us
    unnamed x10, local copies, waits for them, and re-layouts  61.7 us
    psum x1, waiting for transfers between devices, shards(): totals = lax.psum(partial_out, 'fsdp')  59.9 us
    convert_element_type x1, other arithmetic, shards(): update.astype(jnp.bfloat16)  23.6 us
    dot_general x1, matrix products, shards(): products = jnp.dot(gathered, stacked, preferred_element_type=jnp.float32)  16.8 us
    dot_general x1, matrix products, shards(): lax.dot_general(gathered, paired, (((0,), (0,)), ((), ())), preferred_ele...  16 us
  transfers between devices with their start and end apart: 3, of which 2 were waited for; matrix products, arithmetic and copies ran while one was open for 18% of the time, Pallas kernels for 0%

commit v1 on v0

--- a/solution.py
+++ b/solution.py
@@ -18,7 +18,18 @@
 
 
 def shards(hidden_t, down_weight, probe, grad_moment, curv_moment, target):
-    gathered = lax.all_gather(hidden_t, "tensor", axis=1, tiled=True)
+    full_n = lax.axis_size("tensor")
+    series = [hidden_t]
+    q = 0
+    while q < full_n - 1:
+        part_next = lax.ppermute(
+            series[-1], axis_name="tensor", perm=[(i0, (i0 + 1) % full_n) for i0 in range(full_n)]
+        )
+        series.append(part_next)
+        q = q + 1
+    current_value = jnp.concatenate(series[::-1], 1)
+    step_out = lax.axis_index("tensor")
+    gathered = jnp.roll(current_value, (step_out + 1) * hidden_t.shape[1], 1)
     col_width = down_weight.shape[1]
     token_count = gathered.shape[1]
     paired = jnp.concatenate([down_weight, probe], axis=1)

time: 275 us -> 236 us (0.86)
  local copies, waits for them, and re-layouts: 63.2 us -> 16 us
  waiting for transfers between devices: 137 us -> 148 us
  matrix products: 32.8 us -> 29.2 us
  starting transfers between devices: 0.11 us -> 3.16 us
    all_gather x1 -> x0, waiting for transfers between devices: 75.6 us -> none  [shards(): gathered = lax.all_gather(hidden_t, 'tensor', axis=1, tiled=True)]
    ppermute x0 -> x3, waiting for transfers between devices: none -> 68.6 us  [shards(): lax.ppermute(series[-1], axis_name='tensor', perm=[(i0, (i0 + 1) % full_n...]
    unnamed x10 -> x25, local copies, waits for them, and re-layouts: 61.7 us -> 15.1 us
    psum x1, waiting for transfers between devices: 59.9 us -> 78.9 us  [shards(): totals = lax.psum(partial_out, 'fsdp')]
    ppermute x0 -> x3, starting transfers between devices: none -> 3.08 us  [shards(): lax.ppermute(series[-1], axis_name='tensor', perm=[(i0, (i0 + 1) % full_n...]
  transfers between devices with their start and end apart: 3 -> 5, of which waited for: 2 -> 4; matrix products, arithmetic and copies ran while one was open for 18% -> 12% of each run, Pallas kernels for 0% -> 0%
where the time goes in v1:
time: 236 us; the launch traced here: 235 us
  waiting for transfers between devices  148 us (63%)
  matrix products  29.2 us (12%)
  other arithmetic  25.2 us (11%)
  local copies, waits for them, and re-layouts  16 us (7%)
  between operations  14.1 us (6%)
  starting transfers between devices  3.16 us (1%)
    psum x1, waiting for transfers between devices, shards(): totals = lax.psum(partial_out, 'fsdp')  78.9 us
    ppermute x3, waiting for transfers between devices, shards(): lax.ppermute(series[-1], axis_name='tensor', perm=[(i0, (i0 + 1) % full_n...  68.6 us
    convert_element_type x1, other arithmetic, shards(): update.astype(jnp.bfloat16)  20.9 us
    dot_general x1, matrix products, shards(): products = jnp.dot(gathered, stacked, preferred_element_type=jnp.float32)  15.5 us
    unnamed x25, local copies, waits for them, and re-layouts  15.1 us
    dot_general x1, matrix products, shards(): lax.dot_general(gathered, paired, (((0,), (0,)), ((), ())), preferred_ele...  13.7 us
  transfers between devices with their start and end apart: 5, of which 4 were waited for; matrix products, arithmetic and copies ran while one was open for 12% of the time, Pallas kernels for 0%

profile of v1, /device:TPU:0, one launch (start us, length us, event | category | flops | bytes accessed | tf_op | source)
XLA Modules:
  0.0 235.3 jit_solution(6145381642236701387)
XLA Ops:
  7.2 0.0 all-gather.2.cloned.1.call-start
  7.2 3.1 %collective-permute-start = (bf16[3584,128]{1,0:T(8,128)(2,1)}, bf16[3584,128]{1,0:T(8,128)(2,1)S(1)}, u32[]{:S(2)}, u32[]{:S(2)}) collective-permute-start(bf16[3584,128]{1,0:T(8,128)(2,1)} %param.6), channel_id=1, source_target_pairs={{0,1},{1,2},{2,3},{3,0},{4,5},{5,6},{6,7},{7,4},{8,9},{9,10},{10,1... | collective-permute-start | bytes 2752520 | tf_op jit(solution)/shard_map/ppermute | solution.py:25
  10.3 22.6 %collective-permute-done = bf16[3584,128]{1,0:T(8,128)(2,1)S(1)} collective-permute-done((bf16[3584,128]{1,0:T(8,128)(2,1)}, bf16[3584,128]{1,0:T(8,128)(2,1)S(1)}, u32[]{:S(2)}, u32[]{:S(2)}) %collective-permute-start) | collective-permute-done | bytes 917536 | tf_op jit(solution)/shard_map/ppermute | solution.py:25
  32.9 0.0 copy-start.1
  32.9 0.9 copy-done.1
  33.8 0.0 collective-permute-start.1
  33.8 23.4 %collective-permute-done.1 = bf16[3584,128]{1,0:T(8,128)(2,1)} collective-permute-done((bf16[3584,128]{1,0:T(8,128)(2,1)S(1)}, bf16[3584,128]{1,0:T(8,128)(2,1)}, u32[]{:S(2)}, u32[]{:S(2)}) %collective-permute-start.1) | collective-permute-done | bytes 917536 | tf_op jit(solution)/shard_map/ppermute | solution.py:25
  57.2 0.0 collective-permute-start.2
  57.2 0.0 all-gather.2.cloned.1.call-update
  57.3 0.0 all-reduce.2.cloned.1.call-start
  57.3 0.0 slice-start
  57.3 0.0 copy-start.2
  57.4 0.0 copy-start
  57.4 22.6 %collective-permute-done.2 = bf16[3584,128]{1,0:T(8,128)(2,1)} collective-permute-done((bf16[3584,128]{1,0:T(8,128)(2,1)}, bf16[3584,128]{1,0:T(8,128)(2,1)}, u32[]{:S(2)}, u32[]{:S(2)}) %collective-permute-start.2) | collective-permute-done | bytes 917536 | tf_op jit(solution)/shard_map/ppermute | solution.py:25
  80.0 2.2 constant_dynamic-update-slice_fusion.7
  82.1 2.2 constant_dynamic-update-slice_fusion.6
  84.3 2.2 constant_dynamic-update-slice_fusion.5
  86.5 0.0 slice-start.1
  86.5 2.3 constant_dynamic-update-slice_fusion.4
  88.8 2.2 constant_dynamic-update-slice_fusion.3
  90.9 2.2 constant_dynamic-update-slice_fusion.2
  93.1 0.0 copy-done.2
  93.1 1.0 constant_dynamic-update-slice_fusion.1
  94.1 0.0 copy-done
  94.1 1.0 constant_dynamic-update-slice_fusion
  95.1 0.0 slice-done
  95.1 0.0 slice-done.1
  95.1 13.7 %fusion.3 = f32[512,2048]{1,0:T(8,128)} fusion(bf16[3584,1024]{1,0:T(8,128)(2,1)S(1)} %bitcast.1, bf16[3584,1024]{1,0:T(8,128)(2,1)} %param.7, bf16[3584,1024]{1,0:T(8,128)(2,1)} %constant_dynamic-update-slice_fusion, s32[]{:T(128)S(6)} %select_n.14), kind=kOutput, calls=%fused_computation.5 | convolution fusion | flops 7545552896 | bytes 22544388 | tf_op jit(solution)/shard_map/dot_general | solution.py:36
  108.8 0.0 all-reduce.2.cloned.1.call-update
  108.8 0.0 all-gather.2.cloned.1.call-done
  108.8 78.9 %all-reduce.2.cloned.1.call-done = f32[512,2048]{1,0:T(8,128)} async-done(((f32[512,2048]{1,0:T(8,128)}), f32[512,2048]{1,0:T(8,128)}) %all-reduce.2.cloned.1.call-update) | async-done | bytes 4194320 | tf_op jit(solution)/shard_map/psum | solution.py:39
  187.7 0.0 slice-start.2
  187.7 0.0 slice-start.4
  187.7 4.3 %fusion.14 = (bf16[512,1024]{1,0:T(8,128)(2,1)S(1)}, bf16[512,1024]{1,0:T(8,128)(2,1)}) fusion(f32[512,2048]{1,0:T(8,128)} %all-reduce.2.cloned.1.call-done, bf16[512,1024]{1,0:T(8,128)(2,1)} %all-gather.2.cloned.1.call-done), kind=kLoop, calls=%fused_computation.19 | loop fusion | flops 3145728 | bytes 7340032 | tf_op jit(solution)/shard_map/convert_element_type | solution.py:13
  192.0 0.0 slice-start.3
  192.0 0.0 slice-start.5
  192.0 15.5 %fusion.8 = f32[3584,2048]{1,0:T(8,128)} fusion(bf16[3584,1024]{1,0:T(8,128)(2,1)} %constant_dynamic-update-slice_fusion, s32[]{:T(128)S(6)} %select_n.14, bf16[512,1024]{1,0:T(8,128)(2,1)} %get-tuple-element.7, bf16[512,1024]{1,0:T(8,128)(2,1)S(1)} %get-tuple-element.6), kind=kOutput, calls=%fused_computation.11 | convolution fusion | flops 7520387072 | bytes 35127300 | tf_op jit(solution)/shard_map/dot_general | solution.py:42
  207.5 0.0 slice-done.2
  207.5 0.0 slice-done.4
  207.5 0.0 slice-done.3
  207.5 0.0 slice-done.5
  207.5 20.9 %clamp_convert_fusion = (bf16[3584,1024]{1,0:T(8,128)(2,1)}, bf16[3584,1024]{1,0:T(8,128)(2,1)}, bf16[3584,1024]{1,0:T(8,128)(2,1)}) fusion(f32[3584,2048]{1,0:T(8,128)} %fusion.8, bf16[3584,1024]{1,0:T(8,128)(2,1)S(1)} %bitcast.5, bf16[3584,1024]{1,0:T(8,128)(2,1)S(1)} %bitcast.3, bf16[3584,1024]{1,0:T(8,128)(2,1)} %param.10), kind=kLoop, calls=%fused_computation.9 | loop fusion | flops 62390272 | bytes 73400320 | tf_op jit(solution)/shard_map/convert_element_type | solution.py:53
  (3 shorter events, 0.0 us)
Async XLA Ops:
  7.2 101.7 %all-gather.2.cloned.1.call-start = ((), (), s32[]{:S(2)}) async-start(), calls=%async_computation.1 | async-start | bytes 1179648 | tf_op jit(solution)/shard_map/all_gather | solution.py:40
  7.2 25.7 %collective-permute-start = (bf16[3584,128]{1,0:T(8,128)(2,1)}, bf16[3584,128]{1,0:T(8,128)(2,1)S(1)}, u32[]{:S(2)}, u32[]{:S(2)}) collective-permute-start(bf16[3584,128]{1,0:T(8,128)(2,1)} %param.6), channel_id=1, source_target_pairs={{0,1},{1,2},{2,3},{3,0},{4,5},{5,6},{6,7},{7,4},{8,9},{9,10},{10,1... | collective-permute-start | bytes 2752520 | tf_op jit(solution)/shard_map/ppermute | solution.py:25
  32.9 0.9 copy-start.1
  33.8 23.4 %collective-permute-start.1 = (bf16[3584,128]{1,0:T(8,128)(2,1)S(1)}, bf16[3584,128]{1,0:T(8,128)(2,1)}, u32[]{:S(2)}, u32[]{:S(2)}) collective-permute-start(bf16[3584,128]{1,0:T(8,128)(2,1)S(1)} %collective-permute-done), channel_id=1, source_target_pairs={{0,1},{1,2},{2,3},{3,0},{4,5},{5,6},{6,7},{7,4},{8,9},{9,10},{10,1... | collective-permute-start | bytes 2752520 | tf_op jit(solution)/shard_map/ppermute | solution.py:25
  57.2 22.7 %collective-permute-start.2 = (bf16[3584,128]{1,0:T(8,128)(2,1)}, bf16[3584,128]{1,0:T(8,128)(2,1)}, u32[]{:S(2)}, u32[]{:S(2)}) collective-permute-start(bf16[3584,128]{1,0:T(8,128)(2,1)} %collective-permute-done.1), channel_id=1, source_target_pairs={{0,1},{1,2},{2,3},{3,0},{4,5},{5,6},{6,7},{7,4},{8,9},{9,10},{10,1... | collective-permute-start | bytes 2752520 | tf_op jit(solution)/shard_map/ppermute | solution.py:25
  57.3 130.5 %all-reduce.2.cloned.1.call-start = ((), (), s32[]{:S(2)}) async-start(), calls=%async_computation | async-start | bytes 8388608 | tf_op jit(solution)/shard_map/psum | solution.py:39
  57.3 37.7 %slice-start = ((s8[7340032]{0:T(1024)(128)(4,1)}), s8[3145728]{0:T(1024)(128)(4,1)S(1)}, s32[]{:S(2)}) async-start(s8[7340032]{0:T(1024)(128)(4,1)} %bitcast), calls=%async_computation.2 | async-start | bytes 6291456
  57.3 35.7 %copy-start.2 = (bf16[3584,128]{1,0:T(8,128)(2,1)S(1)}, bf16[3584,128]{1,0:T(8,128)(2,1)}, u32[]{:S(2)}) copy-start(bf16[3584,128]{1,0:T(8,128)(2,1)} %copy-done.1) | copy-start | bytes 2752516
  57.4 36.7 %copy-start = (bf16[3584,128]{1,0:T(8,128)(2,1)S(1)}, bf16[3584,128]{1,0:T(8,128)(2,1)}, u32[]{:S(2)}) copy-start(bf16[3584,128]{1,0:T(8,128)(2,1)} %param.6) | copy-start | bytes 2752516
  86.5 8.6 %slice-start.1 = ((s8[7340032]{0:T(1024)(128)(4,1)}), s8[4194304]{0:T(1024)(128)(4,1)S(1)}, s32[]{:S(2)}) async-start(s8[7340032]{0:T(1024)(128)(4,1)} %bitcast), calls=%async_computation.3 | async-start | bytes 8388608
  187.7 19.7 %slice-start.2 = ((s8[7340032]{0:T(1024)(128)(4,1)}), s8[4194304]{0:T(1024)(128)(4,1)S(1)}, s32[]{:S(2)}) async-start(s8[7340032]{0:T(1024)(128)(4,1)} %bitcast.2), calls=%async_computation.4 | async-start | bytes 8388608
  187.7 19.7 %slice-start.4 = ((s8[7340032]{0:T(1024)(128)(4,1)}), s8[4194304]{0:T(1024)(128)(4,1)S(1)}, s32[]{:S(2)}) async-start(s8[7340032]{0:T(1024)(128)(4,1)} %bitcast.4), calls=%async_computation.6 | async-start | bytes 8388608
  192.0 15.5 %slice-start.3 = ((s8[7340032]{0:T(1024)(128)(4,1)}), s8[3145728]{0:T(1024)(128)(4,1)S(1)}, s32[]{:S(2)}) async-start(s8[7340032]{0:T(1024)(128)(4,1)} %bitcast.2), calls=%async_computation.5 | async-start | bytes 6291456
  192.0 15.5 %slice-start.5 = ((s8[7340032]{0:T(1024)(128)(4,1)}), s8[3145728]{0:T(1024)(128)(4,1)S(1)}, s32[]{:S(2)}) async-start(s8[7340032]{0:T(1024)(128)(4,1)} %bitcast.4), calls=%async_computation.7 | async-start | bytes 6291456
Sparse Core Ops, SparseCore 0:
  57.4 24.7 all-gather.1
  108.9 78.7 all-reduce.1
